TPU v7x, 32 devices: a whole 2x2x4 slice. The times are simulated.
32 devices in a mesh: horiz: 8 (over z, y), lev: 4 (over x, core).
Axes of the slice: x: 2, y: 2, z: 4, core: 2. Of those that a mesh axis runs over, the one named last changes fastest.
Arguments:
- control: float32 [64, 32, 4096], P('lev', None, 'horiz'), may hold values from -6 to 6
- members: bfloat16 [64, 4, 32, 4096], P('lev', None, None, 'horiz'), may hold values from -6 to 6
- extinction: float32 [4], replicated, may hold values from 0.5 to 2
- kernels: bfloat16 [4096, 64, 128], P('horiz', 'lev'), may hold values from 0 to 1
- innovation: bfloat16 [4096, 128], P('horiz'), may hold values from -16 to 16
- obs_weight: bfloat16 [4096, 128], P('horiz'), may hold values from 0.25 to 4
- owners: int32 [4096, 1], P('horiz'), may hold values from 0 to 7; in each aligned block of 512 rows (0 to 511, 512 to 1023, ...) at most 128 rows name the same one
- pixel_columns: int32 [4096, 128], P('horiz'), may hold values from 0 to 511
- pixel_counts: int32 [4096], P('horiz'), may hold values from 1 to 128
Outputs:
- gradient: float32 [64, 32, 4096], P('lev', None, 'horiz')
Inputs may be any that keep to these rules, and one draw needn't show every extreme that they name: `owners`: among the 512 blocks of one index of horiz, no owner is named more than 128 times, and in some index's blocks one owner is named exactly 128 times.
All inputs are finite; a program needn't handle non-finite values.
Results may differ from a plain program's by a relative error of at most 0.0037.
Values may be sent and summed in bfloat16 or wider, within the bound.
A program may use at most 128 MiB of HBM per device.

v0:
```python
import math
import jax
import jax.numpy as jnp
from jax import lax
from jax.sharding import PartitionSpec as P

LEV = 64
HALF = 4


def with_halo(value, sides, width):
    for axis, dim in sides:
        devices, length = (lax.axis_size(axis), value.shape[dim])
        up = [(i, (i + 1) % devices) for i in range(devices - 1)]
        down = [(j, i) for i, j in up]
        last = lax.slice_in_dim(value, length - width, length, axis=dim)
        first = lax.slice_in_dim(value, 0, width, axis=dim)
        before = lax.ppermute(last, axis, up)
        after = lax.ppermute(first, axis, down)
        value = jnp.concatenate([before, value, after], axis=dim)
    return value


def level_matrix():
    index_levels = jnp.arange(LEV, dtype=jnp.float32)
    spread = LEV / 8.0
    distance = index_levels[:, None] - index_levels[None, :]
    matrix = jnp.exp(-distance * distance / (2.0 * spread * spread)) / (2.5066283 * spread)
    return matrix.astype(jnp.bfloat16)


def column_taps():
    offsets = jnp.arange(2 * HALF + 1, dtype=jnp.float32) - HALF
    spread = HALF / 2.0
    weights = jnp.exp(-offsets * offsets / (2.0 * spread * spread))
    return weights / jnp.sum(weights)


def smooth_columns(values):
    tap_weights = column_taps()
    span = values.shape[2]
    padded = with_halo(values, (("horiz", 2),), HALF)
    running = jnp.zeros(values.shape, jnp.float32)
    for offset in range(2 * HALF + 1):
        running = running + tap_weights[offset] * padded[:, :, offset : offset + span]
    return running


def evolve_pixels(kernel_rows, picked):
    return jnp.sum(kernel_rows.astype(jnp.float32) * picked, axis=1)


def pixel_misfit(evolved, innov_rows, weight_rows, count_rows):
    pixel_width = evolved.shape[1]
    live_pixels = jnp.arange(pixel_width, dtype=jnp.int32)[None, :] < count_rows[:, None]
    return jnp.where(
        live_pixels,
        weight_rows.astype(jnp.float32) * (evolved - innov_rows.astype(jnp.float32)),
        0.0,
    )


def column_onehot(column_block, col_count):
    return (
        jnp.arange(col_count, dtype=jnp.int32)[:, None, None] == column_block[None, :, :]
    ).astype(jnp.float32)


def body(
    control,
    members,
    extinction,
    kernels,
    innovation,
    obs_weight,
    owners,
    pixel_columns,
    pixel_counts,
):
    lev_local, mem_count, col_count = control.shape
    level_loc = level_matrix()
    first_level = lax.axis_index("lev") * lev_local
    mine_rows = lax.dynamic_slice_in_dim(level_loc, first_level, lev_local, 0)
    mine_cols = lax.dynamic_slice_in_dim(level_loc, first_level, lev_local, 1)
    scale = 1.0 / math.sqrt(mem_count)
    control_b = control.astype(jnp.bfloat16)
    section = mine_rows
    vertical = jnp.einsum(
        "ab,bmc->amc",
        section,
        lax.all_gather(control_b, "lev", axis=0, tiled=True),
        preferred_element_type=jnp.float32,
    )
    increment = smooth_columns(vertical)
    mixed = extinction[0] * members[:, 0].astype(jnp.float32)
    for species in range(1, members.shape[1]):
        mixed = mixed + extinction[species] * members[:, species].astype(jnp.float32)
    column_field = jnp.sum(mixed * increment, axis=1) * scale
    owner_ids = owners[:, 0]
    horiz_count = lax.axis_size("horiz")
    blocks_local = owner_ids.shape[0]
    pixel_width = pixel_columns.shape[1]
    capacity = max(2, 2 * (blocks_local // horiz_count))
    total_slots = horiz_count * capacity
    owner_range = jnp.arange(horiz_count, dtype=jnp.int32)
    belongs = (owner_ids[:, None] == owner_range[None, :]).astype(jnp.float32)
    block_range = jnp.arange(blocks_local, dtype=jnp.int32)
    strictly_lower = (block_range[:, None] > block_range[None, :]).astype(jnp.float32)
    earlier = jnp.dot(strictly_lower, belongs, precision=lax.Precision.HIGHEST)
    slot_index = jnp.sum(earlier * belongs, axis=1).astype(jnp.int32)
    target_slot = owner_ids * capacity + slot_index
    placement = jnp.arange(total_slots, dtype=jnp.int32)[:, None] == target_slot[None, :]
    place_half = placement.astype(jnp.bfloat16)
    kernel_buf = (
        jnp.dot(place_half, kernels.reshape(blocks_local, -1), preferred_element_type=jnp.float32)
        .astype(jnp.bfloat16)
        .reshape((total_slots,) + kernels.shape[1:])
    )
    paired = jnp.stack([innovation, obs_weight], 1).reshape(blocks_local, -1)
    value_buf = (
        jnp.dot(place_half, paired, preferred_element_type=jnp.float32)
        .astype(jnp.bfloat16)
        .reshape(total_slots, 2, pixel_width)
    )
    index_rows = jnp.concatenate([pixel_columns, pixel_counts[:, None]], 1).astype(jnp.float32)
    index_buf = jnp.dot(
        placement.astype(jnp.float32), index_rows, precision=lax.Precision.HIGHEST
    ).astype(jnp.int32)
    column_buf = index_buf[:, :pixel_width]
    count_buf = index_buf[:, pixel_width]
    kernel_in, value_in = (
        lax.all_to_all(kernel_buf, "horiz", split_axis=0, concat_axis=0, tiled=True),
        lax.all_to_all(value_buf, "horiz", split_axis=0, concat_axis=0, tiled=True),
    )
    column_in, count_in = (
        lax.all_to_all(column_buf, "horiz", split_axis=0, concat_axis=0, tiled=True),
        lax.all_to_all(count_buf, "horiz", split_axis=0, concat_axis=0, tiled=True),
    )
    slot_group = math.gcd(total_slots, 64)
    group_count = total_slots // slot_group
    kernel_groups = kernel_in.reshape(group_count, slot_group, lev_local, pixel_width)
    column_groups = column_in.reshape(group_count, slot_group, pixel_width)

    def forward_group(operands):
        kernel_block, column_block = operands
        onehot = column_onehot(column_block, col_count)
        picked = jnp.einsum("ac,cgp->gap", column_field, onehot, precision=lax.Precision.HIGHEST)
        return evolve_pixels(kernel_block, picked)

    local_sums = lax.map(forward_group, (kernel_groups, column_groups)).reshape(
        total_slots, pixel_width
    )
    evolved = lax.psum(local_sums, "lev")
    misfit = pixel_misfit(evolved, value_in[:, 0], value_in[:, 1], count_in)
    misfit_groups = misfit.reshape(group_count, slot_group, pixel_width)

    def adjoint_group(running, operands):
        kernel_block, column_block, misfit_block = operands
        onehot = column_onehot(column_block, col_count)
        contrib = kernel_block.astype(jnp.float32) * misfit_block[:, None, :]
        return (
            running + jnp.einsum("gap,cgp->ac", contrib, onehot, precision=lax.Precision.HIGHEST),
            None,
        )

    field_grad, unused = lax.scan(
        adjoint_group,
        jnp.zeros((lev_local, col_count), jnp.float32),
        (kernel_groups, column_groups, misfit_groups),
    )
    member_grad = mixed * field_grad[:, None, :] * scale
    smoothed_b = smooth_columns(member_grad).astype(jnp.bfloat16)
    section = mine_cols
    adjoint_field = jnp.einsum(
        "ba,bmc->amc",
        section,
        lax.all_gather(smoothed_b, "lev", axis=0, tiled=True),
        preferred_element_type=jnp.float32,
    )
    return control + adjoint_field


def solution(mesh):
    placed = (
        P("lev", None, "horiz"),
        P("lev", None, None, "horiz"),
        P(),
        P("horiz", "lev", None),
        P("horiz", None),
        P("horiz", None),
        P("horiz", None),
        P("horiz", None),
        P("horiz"),
    )
    return jax.shard_map(
        body, mesh=mesh, in_specs=placed, out_specs=P("lev", None, "horiz"), check_vma=False
    )
```

profile of v0, /device:TPU:0, one launch (start us, length us, event | category | flops | bytes accessed | tf_op | source)
XLA Modules:
  0.0 520.4 jit_solution(10034451160661777724)
XLA Ops:
  25.5 8.7 %all-to-all-done.3 = s32[8,128,128]{1,2,0:T(8,128)S(1)} async-done(((s32[8,128,128]{1,2,0:T(8,128)}), s32[8,128,128]{1,2,0:T(8,128)S(1)}, u32[]{:S(2)}, u32[]{:S(2)}) %all-to-all-start.3) | async-done | bytes 524320 | tf_op jit(solution)/shard_map/all_to_all | solution.py:136
  47.7 18.3 %all-gather.3.cloned.1.call-done = bf16[64,32,512]{2,0,1:T(8,128)(2,1)} async-done(((bf16[16,32,512]{2,0,1:T(8,128)(2,1)}), bf16[64,32,512]{2,0,1:T(8,128)(2,1)}) %all-gather.3.cloned.1.call-update) | async-done | bytes 2097168 | tf_op jit(solution)/shard_map/all_gather | solution.py:91
  78.2 12.2 %collective-permute-done.1 = f32[16,32,4]{2,0,1:T(8,128)} collective-permute-done((f32[16,32,4]{2,0,1:T(8,128)}, f32[16,32,4]{2,0,1:T(8,128)}, u32[]{:S(2)}, u32[]{:S(2)}) %collective-permute-start.1) | collective-permute-done | bytes 8224 | tf_op jit(solution)/shard_map/ppermute | solution.py:19
  90.4 13.0 %fusion.47 = (f32[16,512]{1,0:T(8,128)S(1)}, f32[16,1,32,512]{3,0,2,1:T(8,128)S(1)}) fusion(f32[16,32,512]{2,0,1:T(8,128)S(1)} %fusion.82, f32[16,32,4]{2,0,1:T(8,128)} %collective-permute-done.1, f32[16,32,4]{2,0,1:T(8,128)} %collective-permute-done, f32[]{:T(128)} %bitcast.32, f32[]{:T(128)} %bitcast.31, f32[]{:T(128)} %bitcast.30, f32[]{:T(128)} %bitcast.29, ...), kind=kLoop, calls=%fused_computation.82 | loop fusion | flops 9953280 | bytes 4243508 | tf_op jit(solution)/shard_map/reduce_sum | solution.py:98
  103.5 30.8 %all-to-all-done = bf16[1024,16,128]{2,1,0:T(8,128)(2,1)} async-done(((bf16[1024,16,128]{2,1,0:T(8,128)(2,1)}), bf16[1024,16,128]{2,1,0:T(8,128)(2,1)}, u32[]{:S(2)}, u32[]{:S(2)}) %all-to-all-start) | async-done | bytes 4194336 | tf_op jit(solution)/shard_map/all_to_all | solution.py:132
  134.3 19.4 %all-to-all-start.2 = ((bf16[1024,2,128]{2,1,0:T(2,128)(2,1)}), bf16[1024,2,128]{2,1,0:T(2,128)(2,1)S(1)}, u32[]{:S(2)}, u32[]{:S(2)}) async-start(bf16[1024,2,128]{2,1,0:T(2,128)(2,1)} %copy.58), calls=%async_computation.2 | async-start | bytes 1048576 | tf_op jit(solution)/shard_map/all_to_all | solution.py:133
  154.0 123.3 %while.21 = (s32[]{:T(128)}, f32[16,64,128]{2,1,0:T(8,128)}, bf16[16,64,16,128]{3,2,1,0:T(8,128)(2,1)}, s32[16,64,128]{2,1,0:T(8,128)}, f32[16,512]{1,0:T(8,128)S(1)}, /*index=5*/s32[]{:T(128)}) while((s32[]{:T(128)}, f32[16,64,128]{2,1,0:T(8,128)}, bf16[16,64,16,128]{3,2,1,0:T(8,128)(2,1)}, s32[16,64,128]{2,1,0:T(8,128)}, ...), condition=%wide.region_5.6_spmd, body=%wide.region_3.5_spmd.sunk | while | flops 809885696 | bytes 491609 | solution.py:150
  289.5 22.2 %all-reduce.2.cloned.1.call-done = f32[1024,128]{1,0:T(8,128)} async-done(((f32[1024,128]{1,0:T(8,128)}), f32[1024,128]{1,0:T(8,128)}) %all-reduce.2.cloned.1.call-update) | async-done | bytes 524304 | tf_op jit(solution)/shard_map/psum | solution.py:153
  313.1 147.6 %while.22 = (s32[]{:T(128)}, f32[16,512]{1,0:T(8,128)S(1)}, bf16[16,64,16,128]{3,2,1,0:T(8,128)(2,1)}, f32[16,64,128]{2,1,0:T(8,128)S(1)}, s32[16,64,128]{2,1,0:T(8,128)}, /*index=5*/s32[]{:T(128)}, s32[]{:T(128)}) while((s32[]{:T(128)}, f32[16,512]{1,0:T(8,128)S(1)}, bf16[16,64,16,128]{3,2,1,0:T(8,128)(2,1)}, ...), condition=%wide.region_8.9_spmd.clone, body=%wide.region_7.8_spmd.clone.sunk | while | flops 809779200 | bytes 524395 | solution.py:166
  313.9 8.4 %fusion.105 = f32[16,512]{1,0:T(8,128)S(1)} fusion(s32[64,128]{1,0:T(8,128)S(1)} %dynamic-slice_bitcast_fusion.7, f32[64,128]{1,0:T(8,128)S(1)} %dynamic-slice_bitcast_fusion.8, bf16[16,64,16,128]{3,2,1,0:T(8,128)(2,1)} %get-tuple-element.220, s32[]{:T(128)S(6)} %copy.105, f32[16,512]{1,0:T(8,128)S(1)} %get-tuple-element.212, pred[]{:T(512)S(6)} %compare.3), kind=kOutput, calls=%fused_computation.13.clone.1 | convolution fusion | flops 809779200 | bytes 393221 | tf_op jit(solution)/shard_map/while/body/eval_jaxpr/gap,cgp->ac/dot_general | solution.py:162
  323.2 8.4 %fusion.105 = f32[16,512]{1,0:T(8,128)S(1)} fusion(s32[64,128]{1,0:T(8,128)S(1)} %dynamic-slice_bitcast_fusion.7, f32[64,128]{1,0:T(8,128)S(1)} %dynamic-slice_bitcast_fusion.8, bf16[16,64,16,128]{3,2,1,0:T(8,128)(2,1)} %get-tuple-element.220, s32[]{:T(128)S(6)} %copy.105, f32[16,512]{1,0:T(8,128)S(1)} %get-tuple-element.212, pred[]{:T(512)S(6)} %compare.3), kind=kOutput, calls=%fused_computation.13.clone.1 | convolution fusion | flops 809779200 | bytes 393221 | tf_op jit(solution)/shard_map/while/body/eval_jaxpr/gap,cgp->ac/dot_general | solution.py:162
  332.4 8.4 %fusion.105 = f32[16,512]{1,0:T(8,128)S(1)} fusion(s32[64,128]{1,0:T(8,128)S(1)} %dynamic-slice_bitcast_fusion.7, f32[64,128]{1,0:T(8,128)S(1)} %dynamic-slice_bitcast_fusion.8, bf16[16,64,16,128]{3,2,1,0:T(8,128)(2,1)} %get-tuple-element.220, s32[]{:T(128)S(6)} %copy.105, f32[16,512]{1,0:T(8,128)S(1)} %get-tuple-element.212, pred[]{:T(512)S(6)} %compare.3), kind=kOutput, calls=%fused_computation.13.clone.1 | convolution fusion | flops 809779200 | bytes 393221 | tf_op jit(solution)/shard_map/while/body/eval_jaxpr/gap,cgp->ac/dot_general | solution.py:162
  341.6 8.4 %fusion.105 = f32[16,512]{1,0:T(8,128)S(1)} fusion(s32[64,128]{1,0:T(8,128)S(1)} %dynamic-slice_bitcast_fusion.7, f32[64,128]{1,0:T(8,128)S(1)} %dynamic-slice_bitcast_fusion.8, bf16[16,64,16,128]{3,2,1,0:T(8,128)(2,1)} %get-tuple-element.220, s32[]{:T(128)S(6)} %copy.105, f32[16,512]{1,0:T(8,128)S(1)} %get-tuple-element.212, pred[]{:T(512)S(6)} %compare.3), kind=kOutput, calls=%fused_computation.13.clone.1 | convolution fusion | flops 809779200 | bytes 393221 | tf_op jit(solution)/shard_map/while/body/eval_jaxpr/gap,cgp->ac/dot_general | solution.py:162
  350.8 8.4 %fusion.105 = f32[16,512]{1,0:T(8,128)S(1)} fusion(s32[64,128]{1,0:T(8,128)S(1)} %dynamic-slice_bitcast_fusion.7, f32[64,128]{1,0:T(8,128)S(1)} %dynamic-slice_bitcast_fusion.8, bf16[16,64,16,128]{3,2,1,0:T(8,128)(2,1)} %get-tuple-element.220, s32[]{:T(128)S(6)} %copy.105, f32[16,512]{1,0:T(8,128)S(1)} %get-tuple-element.212, pred[]{:T(512)S(6)} %compare.3), kind=kOutput, calls=%fused_computation.13.clone.1 | convolution fusion | flops 809779200 | bytes 393221 | tf_op jit(solution)/shard_map/while/body/eval_jaxpr/gap,cgp->ac/dot_general | solution.py:162
  360.1 8.4 %fusion.105 = f32[16,512]{1,0:T(8,128)S(1)} fusion(s32[64,128]{1,0:T(8,128)S(1)} %dynamic-slice_bitcast_fusion.7, f32[64,128]{1,0:T(8,128)S(1)} %dynamic-slice_bitcast_fusion.8, bf16[16,64,16,128]{3,2,1,0:T(8,128)(2,1)} %get-tuple-element.220, s32[]{:T(128)S(6)} %copy.105, f32[16,512]{1,0:T(8,128)S(1)} %get-tuple-element.212, pred[]{:T(512)S(6)} %compare.3), kind=kOutput, calls=%fused_computation.13.clone.1 | convolution fusion | flops 809779200 | bytes 393221 | tf_op jit(solution)/shard_map/while/body/eval_jaxpr/gap,cgp->ac/dot_general | solution.py:162
  387.7 8.4 %fusion.105 = f32[16,512]{1,0:T(8,128)S(1)} fusion(s32[64,128]{1,0:T(8,128)S(1)} %dynamic-slice_bitcast_fusion.7, f32[64,128]{1,0:T(8,128)S(1)} %dynamic-slice_bitcast_fusion.8, bf16[16,64,16,128]{3,2,1,0:T(8,128)(2,1)} %get-tuple-element.220, s32[]{:T(128)S(6)} %copy.105, f32[16,512]{1,0:T(8,128)S(1)} %get-tuple-element.212, pred[]{:T(512)S(6)} %compare.3), kind=kOutput, calls=%fused_computation.13.clone.1 | convolution fusion | flops 809779200 | bytes 393221 | tf_op jit(solution)/shard_map/while/body/eval_jaxpr/gap,cgp->ac/dot_general | solution.py:162
  397.0 8.4 %fusion.105 = f32[16,512]{1,0:T(8,128)S(1)} fusion(s32[64,128]{1,0:T(8,128)S(1)} %dynamic-slice_bitcast_fusion.7, f32[64,128]{1,0:T(8,128)S(1)} %dynamic-slice_bitcast_fusion.8, bf16[16,64,16,128]{3,2,1,0:T(8,128)(2,1)} %get-tuple-element.220, s32[]{:T(128)S(6)} %copy.105, f32[16,512]{1,0:T(8,128)S(1)} %get-tuple-element.212, pred[]{:T(512)S(6)} %compare.3), kind=kOutput, calls=%fused_computation.13.clone.1 | convolution fusion | flops 809779200 | bytes 393221 | tf_op jit(solution)/shard_map/while/body/eval_jaxpr/gap,cgp->ac/dot_general | solution.py:162
  406.2 8.4 %fusion.105 = f32[16,512]{1,0:T(8,128)S(1)} fusion(s32[64,128]{1,0:T(8,128)S(1)} %dynamic-slice_bitcast_fusion.7, f32[64,128]{1,0:T(8,128)S(1)} %dynamic-slice_bitcast_fusion.8, bf16[16,64,16,128]{3,2,1,0:T(8,128)(2,1)} %get-tuple-element.220, s32[]{:T(128)S(6)} %copy.105, f32[16,512]{1,0:T(8,128)S(1)} %get-tuple-element.212, pred[]{:T(512)S(6)} %compare.3), kind=kOutput, calls=%fused_computation.13.clone.1 | convolution fusion | flops 809779200 | bytes 393221 | tf_op jit(solution)/shard_map/while/body/eval_jaxpr/gap,cgp->ac/dot_general | solution.py:162
  415.4 8.4 %fusion.105 = f32[16,512]{1,0:T(8,128)S(1)} fusion(s32[64,128]{1,0:T(8,128)S(1)} %dynamic-slice_bitcast_fusion.7, f32[64,128]{1,0:T(8,128)S(1)} %dynamic-slice_bitcast_fusion.8, bf16[16,64,16,128]{3,2,1,0:T(8,128)(2,1)} %get-tuple-element.220, s32[]{:T(128)S(6)} %copy.105, f32[16,512]{1,0:T(8,128)S(1)} %get-tuple-element.212, pred[]{:T(512)S(6)} %compare.3), kind=kOutput, calls=%fused_computation.13.clone.1 | convolution fusion | flops 809779200 | bytes 393221 | tf_op jit(solution)/shard_map/while/body/eval_jaxpr/gap,cgp->ac/dot_general | solution.py:162
  424.7 8.4 %fusion.105 = f32[16,512]{1,0:T(8,128)S(1)} fusion(s32[64,128]{1,0:T(8,128)S(1)} %dynamic-slice_bitcast_fusion.7, f32[64,128]{1,0:T(8,128)S(1)} %dynamic-slice_bitcast_fusion.8, bf16[16,64,16,128]{3,2,1,0:T(8,128)(2,1)} %get-tuple-element.220, s32[]{:T(128)S(6)} %copy.105, f32[16,512]{1,0:T(8,128)S(1)} %get-tuple-element.212, pred[]{:T(512)S(6)} %compare.3), kind=kOutput, calls=%fused_computation.13.clone.1 | convolution fusion | flops 809779200 | bytes 393221 | tf_op jit(solution)/shard_map/while/body/eval_jaxpr/gap,cgp->ac/dot_general | solution.py:162
  433.9 8.4 %fusion.105 = f32[16,512]{1,0:T(8,128)S(1)} fusion(s32[64,128]{1,0:T(8,128)S(1)} %dynamic-slice_bitcast_fusion.7, f32[64,128]{1,0:T(8,128)S(1)} %dynamic-slice_bitcast_fusion.8, bf16[16,64,16,128]{3,2,1,0:T(8,128)(2,1)} %get-tuple-element.220, s32[]{:T(128)S(6)} %copy.105, f32[16,512]{1,0:T(8,128)S(1)} %get-tuple-element.212, pred[]{:T(512)S(6)} %compare.3), kind=kOutput, calls=%fused_computation.13.clone.1 | convolution fusion | flops 809779200 | bytes 393221 | tf_op jit(solution)/shard_map/while/body/eval_jaxpr/gap,cgp->ac/dot_general | solution.py:162
  443.1 8.4 %fusion.105 = f32[16,512]{1,0:T(8,128)S(1)} fusion(s32[64,128]{1,0:T(8,128)S(1)} %dynamic-slice_bitcast_fusion.7, f32[64,128]{1,0:T(8,128)S(1)} %dynamic-slice_bitcast_fusion.8, bf16[16,64,16,128]{3,2,1,0:T(8,128)(2,1)} %get-tuple-element.220, s32[]{:T(128)S(6)} %copy.105, f32[16,512]{1,0:T(8,128)S(1)} %get-tuple-element.212, pred[]{:T(512)S(6)} %compare.3), kind=kOutput, calls=%fused_computation.13.clone.1 | convolution fusion | flops 809779200 | bytes 393221 | tf_op jit(solution)/shard_map/while/body/eval_jaxpr/gap,cgp->ac/dot_general | solution.py:162
  476.5 10.4 %fusion.25 = bf16[16,32,512]{2,0,1:T(8,128)(2,1)} fusion(f32[16,32,512]{2,0,1:T(8,128)S(1)} %fusion.71, f32[16,32,4]{2,0,1:T(8,128)} %collective-permute-done.3, f32[16,32,4]{2,0,1:T(8,128)} %collective-permute-done.2, f32[16,1,32,512]{3,0,2,1:T(8,128)S(1)} %get-tuple-element.100, f32[]{:T(128)S(6)} %mul.235, f32[16,512]{1,0:T(8,128)S(1)} %get-tuple-element.60, ...), kind=kLoop, calls=%fused_computation.60 | loop fusion | flops 7077888 | bytes 2670628 | tf_op jit(solution)/shard_map/convert_element_type | solution.py:172
  486.9 23.0 %all-gather.5.cloned.1.call-done = bf16[64,32,512]{2,0,1:T(8,128)(2,1)} async-done(((bf16[16,32,512]{2,0,1:T(8,128)(2,1)}), bf16[64,32,512]{2,0,1:T(8,128)(2,1)}) %all-gather.5.cloned.1.call-update) | async-done | bytes 2097168 | tf_op jit(solution)/shard_map/all_gather | solution.py:177
  (153 shorter events, 238.6 us)
Async XLA Ops:
  6.5 13.2 %copy-start.9 = (bf16[512,16,128]{2,1,0:T(8,128)(2,1)S(1)}, bf16[512,16,128]{2,1,0:T(8,128)(2,1)}, u32[]{:S(2)}) copy-start(bf16[512,16,128]{2,1,0:T(8,128)(2,1)} %param.16) | copy-start | bytes 6291460
  11.5 1.0 copy-start.5
  12.4 21.8 %all-to-all-start.3 = ((s32[8,128,128]{1,2,0:T(8,128)}), s32[8,128,128]{1,2,0:T(8,128)S(1)}, u32[]{:S(2)}, u32[]{:S(2)}) async-start(s32[8,128,128]{1,2,0:T(8,128)} %copy_bitcast_fusion), calls=%async_computation.3 | async-start | bytes 1048576 | tf_op jit(solution)/shard_map/all_to_all | solution.py:136
  34.2 0.8 copy-start.2
  35.0 4.8 copy-start
  35.0 6.2 %copy-start.6 = (bf16[512,128]{1,0:T(8,128)(2,1)S(1)}, bf16[512,128]{1,0:T(8,128)(2,1)}, u32[]{:S(2)}) copy-start(bf16[512,128]{1,0:T(8,128)(2,1)} %param.18) | copy-start | bytes 393220
  35.0 99.3 %all-to-all-start = ((bf16[1024,16,128]{2,1,0:T(8,128)(2,1)}), bf16[1024,16,128]{2,1,0:T(8,128)(2,1)}, u32[]{:S(2)}, u32[]{:S(2)}) async-start(bf16[1024,16,128]{2,1,0:T(8,128)(2,1)} %bitcast.110), calls=%async_computation | async-start | bytes 8388608 | tf_op jit(solution)/shard_map/all_to_all | solution.py:132
  39.7 1.7 copy-start.7
  39.7 6.6 %copy-start.1 = (bf16[16,4,32,512]{3,2,1,0:T(8,128)(2,1)S(1)}, bf16[16,4,32,512]{3,2,1,0:T(8,128)(2,1)}, u32[]{:S(2)}) copy-start(bf16[16,4,32,512]{3,2,1,0:T(8,128)(2,1)} %param.14) | copy-start | bytes 6291460
  39.7 26.3 %all-gather.3.cloned.1.call-start = ((), (), s32[]{:S(2)}) async-start(), calls=%async_computation.4 | async-start | bytes 2621440 | tf_op jit(solution)/shard_map/all_gather | solution.py:91
  47.7 27.7 %copy-start.8 = (f32[4]{0:T(128)S(1)}, f32[4]{0:T(128)}, u32[]{:S(2)}) copy-start(f32[4]{0:T(128)} %param.15) | copy-start | bytes 52
  47.7 28.3 %copy-start.4 = (bf16[1024,256]{0,1:T(8,128)(2,1)S(1)}, bf16[1024,256]{0,1:T(8,128)(2,1)}, u32[]{:S(2)}) copy-start(bf16[1024,256]{0,1:T(8,128)(2,1)} %fusion.18) | copy-start | bytes 1572868
  47.7 29.4 %copy-start.3 = (s32[8,128,128]{1,2,0:T(8,128)S(1)}, s32[8,128,128]{1,2,0:T(8,128)}, u32[]{:S(2)}) copy-start(s32[8,128,128]{1,2,0:T(8,128)} %copy-done.2) | copy-start | bytes 1572868
  68.8 21.6 %collective-permute-start.1 = (f32[16,32,4]{2,0,1:T(8,128)}, f32[16,32,4]{2,0,1:T(8,128)}, u32[]{:S(2)}, u32[]{:S(2)}) collective-permute-start(f32[16,32,4]{2,0,1:T(8,128)} %get-tuple-element.108), channel_id=1, source_target_pairs={{4,0},{8,4},{12,8},{16,12},{20,16},{24,20},{28,24},{5,1},{9,5},{13... | collective-permute-start | bytes 24584 | tf_op jit(solution)/shard_map/ppermute | solution.py:19
  70.1 20.3 %collective-permute-start = (f32[16,32,4]{2,0,1:T(8,128)S(1)}, f32[16,32,4]{2,0,1:T(8,128)}, u32[]{:S(2)}, u32[]{:S(2)}) collective-permute-start(f32[16,32,4]{2,0,1:T(8,128)S(1)} %get-tuple-element.107), channel_id=1, source_target_pairs={{0,4},{4,8},{8,12},{12,16},{16,20},{20,24},{24,28},{1,5},{5,9},{9,... | collective-permute-start | bytes 24584 | tf_op jit(solution)/shard_map/ppermute | solution.py:18
  134.3 143.0 %all-to-all-start.2 = ((bf16[1024,2,128]{2,1,0:T(2,128)(2,1)}), bf16[1024,2,128]{2,1,0:T(2,128)(2,1)S(1)}, u32[]{:S(2)}, u32[]{:S(2)}) async-start(bf16[1024,2,128]{2,1,0:T(2,128)(2,1)} %copy.58), calls=%async_computation.2 | async-start | bytes 1048576 | tf_op jit(solution)/shard_map/all_to_all | solution.py:133
  153.7 158.0 %all-reduce.2.cloned.1.call-start = ((), (), s32[]{:S(2)}) async-start(), calls=%async_computation.5 | async-start | bytes 1048576 | tf_op jit(solution)/shard_map/psum | solution.py:153
  277.3 12.2 %all-to-all-start.1 = ((s32[8,128,1]{1,2,0:T(1,128)}), s32[8,128,1]{1,2,0:T(1,128)S(1)}, u32[]{:S(2)}, u32[]{:S(2)}) async-start(s32[8,128,1]{1,2,0:T(1,128)} %slice_bitcast_fusion.1), calls=%async_computation.1 | async-start | bytes 8192 | tf_op jit(solution)/shard_map/all_to_all | solution.py:137
  283.1 226.8 %all-gather.5.cloned.1.call-start = ((), (), s32[]{:S(2)}) async-start(), calls=%async_computation.6 | async-start | bytes 2621440 | tf_op jit(solution)/shard_map/all_gather | solution.py:177
  461.8 9.1 %collective-permute-start.3 = (f32[16,32,4]{2,0,1:T(8,128)}, f32[16,32,4]{2,0,1:T(8,128)}, u32[]{:S(2)}, u32[]{:S(2)}) collective-permute-start(f32[16,32,4]{2,0,1:T(8,128)} %get-tuple-element.106), channel_id=1, source_target_pairs={{4,0},{8,4},{12,8},{16,12},{20,16},{24,20},{28,24},{5,1},{9,5},{13... | collective-permute-start | bytes 24584 | tf_op jit(solution)/shard_map/ppermute | solution.py:19
  463.0 13.4 %collective-permute-start.2 = (f32[16,32,4]{2,0,1:T(8,128)S(1)}, f32[16,32,4]{2,0,1:T(8,128)}, u32[]{:S(2)}, u32[]{:S(2)}) collective-permute-start(f32[16,32,4]{2,0,1:T(8,128)S(1)} %get-tuple-element.105), channel_id=1, source_target_pairs={{0,4},{4,8},{8,12},{12,16},{16,20},{20,24},{24,28},{1,5},{5,9},{9,... | collective-permute-start | bytes 24584 | tf_op jit(solution)/shard_map/ppermute | solution.py:18
Sparse Core Ops, SparseCore 0:
  42.1 23.8 all-gather.2
  277.4 34.3 all-reduce.1
  487.0 22.7 all-gather.4
where the time goes:
time: 525 us; the launch traced here: 520 us
  matrix products  248 us (47%)
  waiting for transfers between devices  128 us (24%)
  local copies, waits for them, and re-layouts  51.6 us (10%)
  starting transfers between devices  50.5 us (10%)
  other arithmetic  28.7 us (5%)
  between operations  14 us (3%)
    dot_general x16, matrix products, adjoint_group(): jnp.einsum('gap,cgp->ac', contrib, onehot, precision=lax.Precision.HIGHEST)  135 us
    dot_general x16, matrix products, forward_group(): jnp.einsum('ac,cgp->gap', column_field, onehot, precision=lax.Precision.H...  101 us
    all_to_all x1, waiting for transfers between devices, body(): lax.all_to_all(kernel_buf, 'horiz', split_axis=0, concat_axis=0, tiled=True)  30.8 us
    eq x32, local copies, waits for them, and re-layouts, column_onehot(): jnp.arange(col_count, dtype=jnp.int32)[:, None, None]  24.7 us
    all_gather x1, waiting for transfers between devices, body(): lax.all_gather(smoothed_b, 'lev', axis=0, tiled=True)  23 us
    psum x1, waiting for transfers between devices, body(): evolved = lax.psum(local_sums, 'lev')  22.2 us
    all_to_all x1, starting transfers between devices, body(): lax.all_to_all(value_buf, 'horiz', split_axis=0, concat_axis=0, tiled=True)  19.4 us
    all_gather x1, waiting for transfers between devices, body(): lax.all_gather(control_b, 'lev', axis=0, tiled=True)  18.3 us
  transfers between devices with their start and end apart: 11, of which 9 were waited for; matrix products, arithmetic and copies ran while one was open for 30% of the time, Pallas kernels for 0%

commit v1 on v0

--- a/solution.py
+++ b/solution.py
@@ -6,6 +6,34 @@
 
 LEV = 64
 HALF = 4
+
+
+def meet_the_matrix(local_x, out_dim, point):
+    wide_out = local_x.shape
+    formed = local_x.reshape(
+        *wide_out[:out_dim], point, wide_out[out_dim] // point, *wide_out[out_dim + 1 :]
+    )
+    return jnp.moveaxis(formed, out_dim, 0)
+
+
+def keep_up_pieces_all(vector, k_dim):
+    y = list(vector.shape[1:])
+    y[k_dim] *= vector.shape[0]
+    return jnp.moveaxis(vector, 0, k_dim).reshape(y)
+
+
+def _read_steps_all(x0, axis_tag, local, shard_in):
+    mid_arr = lax.axis_size(axis_tag)
+    w2 = lax.axis_index(axis_tag)
+    view_out, finding = (mid_arr, w2)
+    now = meet_the_matrix(x0, local, view_out)
+    seen = [now[finding]]
+    for pp in range(1, view_out):
+        met_up = now[finding ^ pp]
+        seen.append(lax.ppermute(met_up, axis_tag, perm=[(k, k ^ pp) for k in range(view_out)]))
+    all_rows = jnp.stack(seen, 0)
+    now = all_rows[finding ^ jnp.arange(view_out)]
+    return keep_up_pieces_all(now, shard_in)
 
 
 def with_halo(value, sides, width):
@@ -133,7 +161,7 @@
         lax.all_to_all(value_buf, "horiz", split_axis=0, concat_axis=0, tiled=True),
     )
     column_in, count_in = (
-        lax.all_to_all(column_buf, "horiz", split_axis=0, concat_axis=0, tiled=True),
+        _read_steps_all(column_buf, "horiz", 0, shard_in=0),
         lax.all_to_all(count_buf, "horiz", split_axis=0, concat_axis=0, tiled=True),
     )
     slot_group = math.gcd(total_slots, 64)

time: 525 us -> 533 us (1.015)
  local copies, waits for them, and re-layouts: 51.6 us -> 69.2 us
  starting transfers between devices: 50.5 us -> 44.8 us
    ppermute x0 -> x7, waiting for transfers between devices: none -> 62.4 us  [_read_steps_all(): lax.ppermute(met_up, axis_tag, perm=[(k, k ^ pp) for k in range(view_out)])]
    all_to_all x1, waiting for transfers between devices: 30.8 us -> 0.01 us  [body(): lax.all_to_all(kernel_buf, 'horiz', split_axis=0, concat_axis=0, tiled=True)]
    all_gather x1, waiting for transfers between devices: 18.3 us -> 0.01 us  [body(): lax.all_gather(control_b, 'lev', axis=0, tiled=True)]
    all_to_all x1, starting transfers between devices: 19.4 us -> 4.63 us  [body(): lax.all_to_all(value_buf, 'horiz', split_axis=0, concat_axis=0, tiled=True)]
    ppermute x0 -> x7, starting transfers between devices: none -> 14.3 us  [_read_steps_all(): lax.ppermute(met_up, axis_tag, perm=[(k, k ^ pp) for k in range(view_out)])]
    ppermute x2, waiting for transfers between devices: 14.1 us -> 1.95 us  [with_halo(): after = lax.ppermute(first, axis, down)]
    unnamed x24 -> x32, local copies, waits for them, and re-layouts: 5.98 us -> 17.2 us
    all_to_all x1 -> x0, waiting for transfers between devices: 8.7 us -> none  [body(): lax.all_to_all(column_buf, 'horiz', split_axis=0, concat_axis=0, tiled=True)]
  transfers between devices with their start and end apart: 11 -> 17, of which waited for: 9 -> 10; matrix products, arithmetic and copies ran while one was open for 30% -> 32% of each run, Pallas kernels for 0% -> 0%
where the time goes in v1:
time: 533 us; the launch traced here: 529 us
  matrix products  248 us (47%)
  waiting for transfers between devices  124 us (23%)
  local copies, waits for them, and re-layouts  69.2 us (13%)
  starting transfers between devices  44.8 us (8%)
  other arithmetic  28.1 us (5%)
  between operations  14 us (3%)
    dot_general x16, matrix products, adjoint_group(): jnp.einsum('gap,cgp->ac', contrib, onehot, precision=lax.Precision.HIGHEST)  135 us
    dot_general x16, matrix products, forward_group(): jnp.einsum('ac,cgp->gap', column_field, onehot, precision=lax.Precision.H...  101 us
    ppermute x7, waiting for transfers between devices, _read_steps_all(): lax.ppermute(met_up, axis_tag, perm=[(k, k ^ pp) for k in range(view_out)])  62.4 us
    eq x32, local copies, waits for them, and re-layouts, column_onehot(): jnp.arange(col_count, dtype=jnp.int32)[:, None, None]  24.7 us
    all_gather x1, waiting for transfers between devices, body(): lax.all_gather(smoothed_b, 'lev', axis=0, tiled=True)  23 us
    psum x1, waiting for transfers between devices, body(): evolved = lax.psum(local_sums, 'lev')  22.3 us
    unnamed x32, local copies, waits for them, and re-layouts  17.2 us
    ppermute x7, starting transfers between devices, _read_steps_all(): lax.ppermute(met_up, axis_tag, perm=[(k, k ^ pp) for k in range(view_out)])  14.3 us
  transfers between devices with their start and end apart: 17, of which 10 were waited for; matrix products, arithmetic and copies ran while one was open for 32% of the time, Pallas kernels for 0%

profile of v1, /device:TPU:0, one launch (start us, length us, event | category | flops | bytes accessed | tf_op | source)
XLA Modules:
  0.0 528.6 jit_solution(10550397455923203279)
XLA Ops:
  63.1 31.2 %collective-permute-done.1 = s32[128,128]{1,0:T(8,128)} collective-permute-done((s32[128,128]{1,0:T(8,128)}, s32[128,128]{1,0:T(8,128)}, u32[]{:S(2)}, u32[]{:S(2)}) %collective-permute-start.1) | collective-permute-done | bytes 65568 | tf_op jit(solution)/shard_map/ppermute | solution.py:33
  101.0 23.7 %collective-permute-done.3 = s32[128,128]{1,0:T(8,128)} collective-permute-done((s32[128,128]{1,0:T(8,128)}, s32[128,128]{1,0:T(8,128)}, u32[]{:S(2)}, u32[]{:S(2)}) %collective-permute-start.3) | collective-permute-done | bytes 65568 | tf_op jit(solution)/shard_map/ppermute | solution.py:33
  144.5 12.7 %fusion.47 = (f32[16,512]{1,0:T(8,128)S(1)}, f32[16,1,32,512]{3,0,2,1:T(8,128)S(1)}) fusion(f32[16,32,512]{2,0,1:T(8,128)S(1)} %fusion.82, f32[16,32,4]{2,0,1:T(8,128)S(1)} %collective-permute-done.8, f32[16,32,4]{2,0,1:T(8,128)} %copy-done.3, f32[]{:T(128)} %bitcast.47, f32[]{:T(128)} %bitcast.46, f32[]{:T(128)} %bitcast.45, f32[]{:T(128)} %bitcast.44, ...), kind=kLoop, calls=%fused_computation.83 | loop fusion | flops 9953280 | bytes 4243508 | tf_op jit(solution)/shard_map/reduce_sum | solution.py:126
  162.0 123.4 %while.21 = (s32[]{:T(128)}, f32[16,64,128]{2,1,0:T(8,128)}, bf16[16,64,16,128]{3,2,1,0:T(8,128)(2,1)}, s32[16,64,128]{2,1,0:T(8,128)}, f32[16,512]{1,0:T(8,128)S(1)}, /*index=5*/s32[]{:T(128)}) while((s32[]{:T(128)}, f32[16,64,128]{2,1,0:T(8,128)}, bf16[16,64,16,128]{3,2,1,0:T(8,128)(2,1)}, s32[16,64,128]{2,1,0:T(8,128)}, ...), condition=%wide.region_5.6_spmd, body=%wide.region_3.5_spmd.sunk | while | flops 809885696 | bytes 491609 | solution.py:178
  297.7 22.3 %all-reduce.2.cloned.1.call-done = f32[1024,128]{1,0:T(8,128)} async-done(((f32[1024,128]{1,0:T(8,128)}), f32[1024,128]{1,0:T(8,128)}) %all-reduce.2.cloned.1.call-update) | async-done | bytes 524304 | tf_op jit(solution)/shard_map/psum | solution.py:181
  321.4 147.6 %while.22 = (s32[]{:T(128)}, f32[16,512]{1,0:T(8,128)S(1)}, bf16[16,64,16,128]{3,2,1,0:T(8,128)(2,1)}, f32[16,64,128]{2,1,0:T(8,128)S(1)}, s32[16,64,128]{2,1,0:T(8,128)}, /*index=5*/s32[]{:T(128)}, s32[]{:T(128)}) while((s32[]{:T(128)}, f32[16,512]{1,0:T(8,128)S(1)}, bf16[16,64,16,128]{3,2,1,0:T(8,128)(2,1)}, ...), condition=%wide.region_8.9_spmd.clone, body=%wide.region_7.8_spmd.clone.sunk | while | flops 809779200 | bytes 524395 | solution.py:194
  322.2 8.4 %fusion.106 = f32[16,512]{1,0:T(8,128)S(1)} fusion(s32[64,128]{1,0:T(8,128)S(1)} %dynamic-slice_bitcast_fusion.7, f32[64,128]{1,0:T(8,128)S(1)} %dynamic-slice_bitcast_fusion.8, bf16[16,64,16,128]{3,2,1,0:T(8,128)(2,1)} %get-tuple-element.228, s32[]{:T(128)S(6)} %copy.110, f32[16,512]{1,0:T(8,128)S(1)} %get-tuple-element.220, pred[]{:T(512)S(6)} %compare.3), kind=kOutput, calls=%fused_computation.14.clone.1 | convolution fusion | flops 809779200 | bytes 393221 | tf_op jit(solution)/shard_map/while/body/eval_jaxpr/gap,cgp->ac/dot_general | solution.py:190
  331.4 8.4 %fusion.106 = f32[16,512]{1,0:T(8,128)S(1)} fusion(s32[64,128]{1,0:T(8,128)S(1)} %dynamic-slice_bitcast_fusion.7, f32[64,128]{1,0:T(8,128)S(1)} %dynamic-slice_bitcast_fusion.8, bf16[16,64,16,128]{3,2,1,0:T(8,128)(2,1)} %get-tuple-element.228, s32[]{:T(128)S(6)} %copy.110, f32[16,512]{1,0:T(8,128)S(1)} %get-tuple-element.220, pred[]{:T(512)S(6)} %compare.3), kind=kOutput, calls=%fused_computation.14.clone.1 | convolution fusion | flops 809779200 | bytes 393221 | tf_op jit(solution)/shard_map/while/body/eval_jaxpr/gap,cgp->ac/dot_general | solution.py:190
  340.7 8.4 %fusion.106 = f32[16,512]{1,0:T(8,128)S(1)} fusion(s32[64,128]{1,0:T(8,128)S(1)} %dynamic-slice_bitcast_fusion.7, f32[64,128]{1,0:T(8,128)S(1)} %dynamic-slice_bitcast_fusion.8, bf16[16,64,16,128]{3,2,1,0:T(8,128)(2,1)} %get-tuple-element.228, s32[]{:T(128)S(6)} %copy.110, f32[16,512]{1,0:T(8,128)S(1)} %get-tuple-element.220, pred[]{:T(512)S(6)} %compare.3), kind=kOutput, calls=%fused_computation.14.clone.1 | convolution fusion | flops 809779200 | bytes 393221 | tf_op jit(solution)/shard_map/while/body/eval_jaxpr/gap,cgp->ac/dot_general | solution.py:190
  349.9 8.4 %fusion.106 = f32[16,512]{1,0:T(8,128)S(1)} fusion(s32[64,128]{1,0:T(8,128)S(1)} %dynamic-slice_bitcast_fusion.7, f32[64,128]{1,0:T(8,128)S(1)} %dynamic-slice_bitcast_fusion.8, bf16[16,64,16,128]{3,2,1,0:T(8,128)(2,1)} %get-tuple-element.228, s32[]{:T(128)S(6)} %copy.110, f32[16,512]{1,0:T(8,128)S(1)} %get-tuple-element.220, pred[]{:T(512)S(6)} %compare.3), kind=kOutput, calls=%fused_computation.14.clone.1 | convolution fusion | flops 809779200 | bytes 393221 | tf_op jit(solution)/shard_map/while/body/eval_jaxpr/gap,cgp->ac/dot_general | solution.py:190
  359.1 8.4 %fusion.106 = f32[16,512]{1,0:T(8,128)S(1)} fusion(s32[64,128]{1,0:T(8,128)S(1)} %dynamic-slice_bitcast_fusion.7, f32[64,128]{1,0:T(8,128)S(1)} %dynamic-slice_bitcast_fusion.8, bf16[16,64,16,128]{3,2,1,0:T(8,128)(2,1)} %get-tuple-element.228, s32[]{:T(128)S(6)} %copy.110, f32[16,512]{1,0:T(8,128)S(1)} %get-tuple-element.220, pred[]{:T(512)S(6)} %compare.3), kind=kOutput, calls=%fused_computation.14.clone.1 | convolution fusion | flops 809779200 | bytes 393221 | tf_op jit(solution)/shard_map/while/body/eval_jaxpr/gap,cgp->ac/dot_general | solution.py:190
  368.3 8.4 %fusion.106 = f32[16,512]{1,0:T(8,128)S(1)} fusion(s32[64,128]{1,0:T(8,128)S(1)} %dynamic-slice_bitcast_fusion.7, f32[64,128]{1,0:T(8,128)S(1)} %dynamic-slice_bitcast_fusion.8, bf16[16,64,16,128]{3,2,1,0:T(8,128)(2,1)} %get-tuple-element.228, s32[]{:T(128)S(6)} %copy.110, f32[16,512]{1,0:T(8,128)S(1)} %get-tuple-element.220, pred[]{:T(512)S(6)} %compare.3), kind=kOutput, calls=%fused_computation.14.clone.1 | convolution fusion | flops 809779200 | bytes 393221 | tf_op jit(solution)/shard_map/while/body/eval_jaxpr/gap,cgp->ac/dot_general | solution.py:190
  377.6 8.4 %fusion.106 = f32[16,512]{1,0:T(8,128)S(1)} fusion(s32[64,128]{1,0:T(8,128)S(1)} %dynamic-slice_bitcast_fusion.7, f32[64,128]{1,0:T(8,128)S(1)} %dynamic-slice_bitcast_fusion.8, bf16[16,64,16,128]{3,2,1,0:T(8,128)(2,1)} %get-tuple-element.228, s32[]{:T(128)S(6)} %copy.110, f32[16,512]{1,0:T(8,128)S(1)} %get-tuple-element.220, pred[]{:T(512)S(6)} %compare.3), kind=kOutput, calls=%fused_computation.14.clone.1 | convolution fusion | flops 809779200 | bytes 393221 | tf_op jit(solution)/shard_map/while/body/eval_jaxpr/gap,cgp->ac/dot_general | solution.py:190
  386.8 8.4 %fusion.106 = f32[16,512]{1,0:T(8,128)S(1)} fusion(s32[64,128]{1,0:T(8,128)S(1)} %dynamic-slice_bitcast_fusion.7, f32[64,128]{1,0:T(8,128)S(1)} %dynamic-slice_bitcast_fusion.8, bf16[16,64,16,128]{3,2,1,0:T(8,128)(2,1)} %get-tuple-element.228, s32[]{:T(128)S(6)} %copy.110, f32[16,512]{1,0:T(8,128)S(1)} %get-tuple-element.220, pred[]{:T(512)S(6)} %compare.3), kind=kOutput, calls=%fused_computation.14.clone.1 | convolution fusion | flops 809779200 | bytes 393221 | tf_op jit(solution)/shard_map/while/body/eval_jaxpr/gap,cgp->ac/dot_general | solution.py:190
  396.0 8.4 %fusion.106 = f32[16,512]{1,0:T(8,128)S(1)} fusion(s32[64,128]{1,0:T(8,128)S(1)} %dynamic-slice_bitcast_fusion.7, f32[64,128]{1,0:T(8,128)S(1)} %dynamic-slice_bitcast_fusion.8, bf16[16,64,16,128]{3,2,1,0:T(8,128)(2,1)} %get-tuple-element.228, s32[]{:T(128)S(6)} %copy.110, f32[16,512]{1,0:T(8,128)S(1)} %get-tuple-element.220, pred[]{:T(512)S(6)} %compare.3), kind=kOutput, calls=%fused_computation.14.clone.1 | convolution fusion | flops 809779200 | bytes 393221 | tf_op jit(solution)/shard_map/while/body/eval_jaxpr/gap,cgp->ac/dot_general | solution.py:190
  405.2 8.4 %fusion.106 = f32[16,512]{1,0:T(8,128)S(1)} fusion(s32[64,128]{1,0:T(8,128)S(1)} %dynamic-slice_bitcast_fusion.7, f32[64,128]{1,0:T(8,128)S(1)} %dynamic-slice_bitcast_fusion.8, bf16[16,64,16,128]{3,2,1,0:T(8,128)(2,1)} %get-tuple-element.228, s32[]{:T(128)S(6)} %copy.110, f32[16,512]{1,0:T(8,128)S(1)} %get-tuple-element.220, pred[]{:T(512)S(6)} %compare.3), kind=kOutput, calls=%fused_computation.14.clone.1 | convolution fusion | flops 809779200 | bytes 393221 | tf_op jit(solution)/shard_map/while/body/eval_jaxpr/gap,cgp->ac/dot_general | solution.py:190
  414.5 8.4 %fusion.106 = f32[16,512]{1,0:T(8,128)S(1)} fusion(s32[64,128]{1,0:T(8,128)S(1)} %dynamic-slice_bitcast_fusion.7, f32[64,128]{1,0:T(8,128)S(1)} %dynamic-slice_bitcast_fusion.8, bf16[16,64,16,128]{3,2,1,0:T(8,128)(2,1)} %get-tuple-element.228, s32[]{:T(128)S(6)} %copy.110, f32[16,512]{1,0:T(8,128)S(1)} %get-tuple-element.220, pred[]{:T(512)S(6)} %compare.3), kind=kOutput, calls=%fused_computation.14.clone.1 | convolution fusion | flops 809779200 | bytes 393221 | tf_op jit(solution)/shard_map/while/body/eval_jaxpr/gap,cgp->ac/dot_general | solution.py:190
  423.7 8.4 %fusion.106 = f32[16,512]{1,0:T(8,128)S(1)} fusion(s32[64,128]{1,0:T(8,128)S(1)} %dynamic-slice_bitcast_fusion.7, f32[64,128]{1,0:T(8,128)S(1)} %dynamic-slice_bitcast_fusion.8, bf16[16,64,16,128]{3,2,1,0:T(8,128)(2,1)} %get-tuple-element.228, s32[]{:T(128)S(6)} %copy.110, f32[16,512]{1,0:T(8,128)S(1)} %get-tuple-element.220, pred[]{:T(512)S(6)} %compare.3), kind=kOutput, calls=%fused_computation.14.clone.1 | convolution fusion | flops 809779200 | bytes 393221 | tf_op jit(solution)/shard_map/while/body/eval_jaxpr/gap,cgp->ac/dot_general | solution.py:190
  432.9 8.4 %fusion.106 = f32[16,512]{1,0:T(8,128)S(1)} fusion(s32[64,128]{1,0:T(8,128)S(1)} %dynamic-slice_bitcast_fusion.7, f32[64,128]{1,0:T(8,128)S(1)} %dynamic-slice_bitcast_fusion.8, bf16[16,64,16,128]{3,2,1,0:T(8,128)(2,1)} %get-tuple-element.228, s32[]{:T(128)S(6)} %copy.110, f32[16,512]{1,0:T(8,128)S(1)} %get-tuple-element.220, pred[]{:T(512)S(6)} %compare.3), kind=kOutput, calls=%fused_computation.14.clone.1 | convolution fusion | flops 809779200 | bytes 393221 | tf_op jit(solution)/shard_map/while/body/eval_jaxpr/gap,cgp->ac/dot_general | solution.py:190
  442.1 8.4 %fusion.106 = f32[16,512]{1,0:T(8,128)S(1)} fusion(s32[64,128]{1,0:T(8,128)S(1)} %dynamic-slice_bitcast_fusion.7, f32[64,128]{1,0:T(8,128)S(1)} %dynamic-slice_bitcast_fusion.8, bf16[16,64,16,128]{3,2,1,0:T(8,128)(2,1)} %get-tuple-element.228, s32[]{:T(128)S(6)} %copy.110, f32[16,512]{1,0:T(8,128)S(1)} %get-tuple-element.220, pred[]{:T(512)S(6)} %compare.3), kind=kOutput, calls=%fused_computation.14.clone.1 | convolution fusion | flops 809779200 | bytes 393221 | tf_op jit(solution)/shard_map/while/body/eval_jaxpr/gap,cgp->ac/dot_general | solution.py:190
  451.4 8.4 %fusion.106 = f32[16,512]{1,0:T(8,128)S(1)} fusion(s32[64,128]{1,0:T(8,128)S(1)} %dynamic-slice_bitcast_fusion.7, f32[64,128]{1,0:T(8,128)S(1)} %dynamic-slice_bitcast_fusion.8, bf16[16,64,16,128]{3,2,1,0:T(8,128)(2,1)} %get-tuple-element.228, s32[]{:T(128)S(6)} %copy.110, f32[16,512]{1,0:T(8,128)S(1)} %get-tuple-element.220, pred[]{:T(512)S(6)} %compare.3), kind=kOutput, calls=%fused_computation.14.clone.1 | convolution fusion | flops 809779200 | bytes 393221 | tf_op jit(solution)/shard_map/while/body/eval_jaxpr/gap,cgp->ac/dot_general | solution.py:190
  460.6 8.4 %fusion.106 = f32[16,512]{1,0:T(8,128)S(1)} fusion(s32[64,128]{1,0:T(8,128)S(1)} %dynamic-slice_bitcast_fusion.7, f32[64,128]{1,0:T(8,128)S(1)} %dynamic-slice_bitcast_fusion.8, bf16[16,64,16,128]{3,2,1,0:T(8,128)(2,1)} %get-tuple-element.228, s32[]{:T(128)S(6)} %copy.110, f32[16,512]{1,0:T(8,128)S(1)} %get-tuple-element.220, pred[]{:T(512)S(6)} %compare.3), kind=kOutput, calls=%fused_computation.14.clone.1 | convolution fusion | flops 809779200 | bytes 393221 | tf_op jit(solution)/shard_map/while/body/eval_jaxpr/gap,cgp->ac/dot_general | solution.py:190
  484.7 10.3 %fusion.25 = bf16[16,32,512]{2,0,1:T(8,128)(2,1)} fusion(f32[16,32,512]{2,0,1:T(8,128)S(1)} %fusion.71, f32[16,32,4]{2,0,1:T(8,128)} %collective-permute-done.10, f32[16,32,4]{2,0,1:T(8,128)} %collective-permute-done.9, f32[16,1,32,512]{3,0,2,1:T(8,128)S(1)} %get-tuple-element.100, f32[]{:T(128)S(6)} %mul.235, f32[16,512]{1,0:T(8,128)S(1)} %get-tuple-element.60, ...), kind=kLoop, calls=%fused_computation.61 | loop fusion | flops 7077888 | bytes 2670628 | tf_op jit(solution)/shard_map/convert_element_type | solution.py:200
  495.1 23.0 %all-gather.5.cloned.1.call-done = bf16[64,32,512]{2,0,1:T(8,128)(2,1)} async-done(((bf16[16,32,512]{2,0,1:T(8,128)(2,1)}), bf16[64,32,512]{2,0,1:T(8,128)(2,1)}) %all-gather.5.cloned.1.call-update) | async-done | bytes 2097168 | tf_op jit(solution)/shard_map/all_gather | solution.py:205
  (183 shorter events, 256.3 us)
Async XLA Ops:
  15.6 7.5 %copy-start = (f32[16,32,512]{2,1,0:T(8,128)S(1)}, f32[16,32,512]{2,1,0:T(8,128)}, u32[]{:S(2)}) copy-start(f32[16,32,512]{2,1,0:T(8,128)} %param.13) | copy-start | bytes 3145732
  15.6 141.5 %all-to-all-start = ((bf16[1024,16,128]{2,1,0:T(8,128)(2,1)}), bf16[1024,16,128]{2,1,0:T(8,128)(2,1)}, u32[]{:S(2)}, u32[]{:S(2)}) async-start(bf16[1024,16,128]{2,1,0:T(8,128)(2,1)} %bitcast.133), calls=%async_computation | async-start | bytes 8388608 | tf_op jit(solution)/shard_map/all_to_all | solution.py:160
  23.0 1.5 copy-start.7
  23.0 1.7 copy-start.8
  23.1 105.8 %all-gather.3.cloned.1.call-start = ((), (), s32[]{:S(2)}) async-start(), calls=%async_computation.3 | async-start | bytes 2621440 | tf_op jit(solution)/shard_map/all_gather | solution.py:119
  28.2 30.8 %collective-permute-start = (s32[128,128]{1,0:T(8,128)}, s32[128,128]{1,0:T(8,128)}, u32[]{:S(2)}, u32[]{:S(2)}) collective-permute-start(s32[128,128]{1,0:T(8,128)} %bitcast.23), channel_id=1, source_target_pairs={{0,4},{4,0},{8,12},{12,8},{16,20},{20,16},{24,28},{28,24},{1,5},{5... | collective-permute-start | bytes 196616 | tf_op jit(solution)/shard_map/ppermute | solution.py:33
  30.9 63.5 %collective-permute-start.1 = (s32[128,128]{1,0:T(8,128)}, s32[128,128]{1,0:T(8,128)}, u32[]{:S(2)}, u32[]{:S(2)}) collective-permute-start(s32[128,128]{1,0:T(8,128)} %bitcast.25), channel_id=1, source_target_pairs={{0,8},{4,12},{8,0},{12,4},{16,24},{20,28},{24,16},{28,20},{1,9},{5... | collective-permute-start | bytes 196616 | tf_op jit(solution)/shard_map/ppermute | solution.py:33
  33.1 66.5 %collective-permute-start.2 = (s32[128,128]{1,0:T(8,128)}, s32[128,128]{1,0:T(8,128)}, u32[]{:S(2)}, u32[]{:S(2)}) collective-permute-start(s32[128,128]{1,0:T(8,128)} %bitcast.27), channel_id=1, source_target_pairs={{0,12},{4,8},{8,4},{12,0},{16,28},{20,24},{24,20},{28,16},{1,13},{... | collective-permute-start | bytes 196616 | tf_op jit(solution)/shard_map/ppermute | solution.py:33
  33.8 90.9 %collective-permute-start.3 = (s32[128,128]{1,0:T(8,128)}, s32[128,128]{1,0:T(8,128)}, u32[]{:S(2)}, u32[]{:S(2)}) collective-permute-start(s32[128,128]{1,0:T(8,128)} %bitcast.29), channel_id=1, source_target_pairs={{0,16},{4,20},{8,24},{12,28},{16,0},{20,4},{24,8},{28,12},{1,17},{... | collective-permute-start | bytes 196616 | tf_op jit(solution)/shard_map/ppermute | solution.py:33
  36.8 10.5 %copy-start.6 = (f32[4]{0:T(128)S(1)}, f32[4]{0:T(128)}, u32[]{:S(2)}) copy-start(f32[4]{0:T(128)} %param.15) | copy-start | bytes 52
  37.5 89.3 %collective-permute-start.4 = (s32[128,128]{1,0:T(8,128)}, s32[128,128]{1,0:T(8,128)}, u32[]{:S(2)}, u32[]{:S(2)}) collective-permute-start(s32[128,128]{1,0:T(8,128)} %bitcast.31), channel_id=1, source_target_pairs={{0,20},{4,16},{8,28},{12,24},{16,4},{20,0},{24,12},{28,8},{1,21},{... | collective-permute-start | bytes 196616 | tf_op jit(solution)/shard_map/ppermute | solution.py:33
  38.9 11.7 %copy-start.1 = (bf16[16,4,32,512]{3,2,1,0:T(8,128)(2,1)S(1)}, bf16[16,4,32,512]{3,2,1,0:T(8,128)(2,1)}, u32[]{:S(2)}) copy-start(bf16[16,4,32,512]{3,2,1,0:T(8,128)(2,1)} %param.14) | copy-start | bytes 6291460
  50.6 8.3 %copy-start.5 = (s32[1,128,128]{2,1,0:T(8,128)S(1)}, s32[1,128,128]{2,1,0:T(8,128)}, u32[]{:S(2)}) copy-start(s32[1,128,128]{2,1,0:T(8,128)} %copy.58) | copy-start | bytes 196612
  50.6 43.7 %copy-start.4 = (s32[1,128,128]{2,1,0:T(8,128)S(1)}, s32[1,128,128]{2,1,0:T(8,128)}, u32[]{:S(2)}) copy-start(s32[1,128,128]{2,1,0:T(8,128)} %copy.59) | copy-start | bytes 196612
  59.0 69.2 %collective-permute-start.5 = (s32[128,128]{1,0:T(8,128)S(1)}, s32[128,128]{1,0:T(8,128)S(1)}, u32[]{:S(2)}, u32[]{:S(2)}) collective-permute-start(s32[128,128]{1,0:T(8,128)S(1)} %bitcast.144), channel_id=1, source_target_pairs={{0,24},{4,28},{8,16},{12,20},{16,8},{20,12},{24,0},{28,4},{1,25},{... | collective-permute-start | bytes 196616 | tf_op jit(solution)/shard_map/ppermute | solution.py:33
  94.4 42.5 %collective-permute-start.6 = (s32[128,128]{1,0:T(8,128)S(1)}, s32[128,128]{1,0:T(8,128)S(1)}, u32[]{:S(2)}, u32[]{:S(2)}) collective-permute-start(s32[128,128]{1,0:T(8,128)S(1)} %bitcast.143), channel_id=1, source_target_pairs={{0,28},{4,24},{8,20},{12,16},{16,12},{20,8},{24,4},{28,0},{1,29},{... | collective-permute-start | bytes 196616 | tf_op jit(solution)/shard_map/ppermute | solution.py:33
  131.0 9.0 %collective-permute-start.8 = (f32[16,32,4]{2,0,1:T(8,128)S(1)}, f32[16,32,4]{2,0,1:T(8,128)S(1)}, u32[]{:S(2)}, u32[]{:S(2)}) collective-permute-start(f32[16,32,4]{2,0,1:T(8,128)S(1)} %get-tuple-element.108), channel_id=1, source_target_pairs={{4,0},{8,4},{12,8},{16,12},{20,16},{24,20},{28,24},{5,1},{9,5},{13... | collective-permute-start | bytes 24584 | tf_op jit(solution)/shard_map/ppermute | solution.py:47
  132.3 11.5 %collective-permute-start.7 = (f32[16,32,4]{2,0,1:T(8,128)S(1)}, f32[16,32,4]{2,0,1:T(8,128)S(1)}, u32[]{:S(2)}, u32[]{:S(2)}) collective-permute-start(f32[16,32,4]{2,0,1:T(8,128)S(1)} %get-tuple-element.107), channel_id=1, source_target_pairs={{0,4},{4,8},{8,12},{12,16},{16,20},{20,24},{24,28},{1,5},{5,9},{9,... | collective-permute-start | bytes 24584 | tf_op jit(solution)/shard_map/ppermute | solution.py:46
  157.2 128.3 %all-to-all-start.2 = ((bf16[1024,2,128]{2,1,0:T(2,128)(2,1)}), bf16[1024,2,128]{2,1,0:T(2,128)(2,1)S(1)}, u32[]{:S(2)}, u32[]{:S(2)}) async-start(bf16[1024,2,128]{2,1,0:T(2,128)(2,1)} %copy.50), calls=%async_computation.2 | async-start | bytes 1048576 | tf_op jit(solution)/shard_map/all_to_all | solution.py:161
  161.8 158.2 %all-reduce.2.cloned.1.call-start = ((), (), s32[]{:S(2)}) async-start(), calls=%async_computation.4 | async-start | bytes 1048576 | tf_op jit(solution)/shard_map/psum | solution.py:181
  285.5 12.2 %all-to-all-start.1 = ((s32[8,128,1]{1,2,0:T(1,128)}), s32[8,128,1]{1,2,0:T(1,128)S(1)}, u32[]{:S(2)}, u32[]{:S(2)}) async-start(s32[8,128,1]{1,2,0:T(1,128)} %slice_bitcast_fusion.1), calls=%async_computation.1 | async-start | bytes 8192 | tf_op jit(solution)/shard_map/all_to_all | solution.py:165
  291.3 226.8 %all-gather.5.cloned.1.call-start = ((), (), s32[]{:S(2)}) async-start(), calls=%async_computation.5 | async-start | bytes 2621440 | tf_op jit(solution)/shard_map/all_gather | solution.py:205
  470.0 9.1 %collective-permute-start.10 = (f32[16,32,4]{2,0,1:T(8,128)}, f32[16,32,4]{2,0,1:T(8,128)}, u32[]{:S(2)}, u32[]{:S(2)}) collective-permute-start(f32[16,32,4]{2,0,1:T(8,128)} %get-tuple-element.106), channel_id=1, source_target_pairs={{4,0},{8,4},{12,8},{16,12},{20,16},{24,20},{28,24},{5,1},{9,5},{13... | collective-permute-start | bytes 24584 | tf_op jit(solution)/shard_map/ppermute | solution.py:47
  471.3 13.4 %collective-permute-start.9 = (f32[16,32,4]{2,0,1:T(8,128)S(1)}, f32[16,32,4]{2,0,1:T(8,128)}, u32[]{:S(2)}, u32[]{:S(2)}) collective-permute-start(f32[16,32,4]{2,0,1:T(8,128)S(1)} %get-tuple-element.105), channel_id=1, source_target_pairs={{0,4},{4,8},{8,12},{12,16},{16,20},{20,24},{24,28},{1,5},{5,9},{9,... | collective-permute-start | bytes 24584 | tf_op jit(solution)/shard_map/ppermute | solution.py:46
  (2 other events, 1.5 us)
Sparse Core Ops, SparseCore 0:
  25.5 23.9 all-gather.2
  285.6 34.3 all-reduce.1
  495.2 22.7 all-gather.4
